TPU v7x, 128 devices: a whole 4x4x4 slice. The times are simulated.
128 devices in a mesh: row: 32 (over x, y_hi, z), col: 4 (over y_lo, core).
Axes of the slice: x: 4, y: 4 (y_hi: 2, y_lo: 2; y = y_hi * 2 + y_lo), z: 4, core: 2. Of those that a mesh axis runs over, the one named last changes fastest.
Arguments:
- image: bfloat16 [1024, 512, 256], P('row', 'col'), may hold values from -6 to 6
- w_expand: bfloat16 [256, 1024], replicated, may hold values from -0.375 to 0.375
- depth_kernel: bfloat16 [3, 3, 1024], replicated, may hold values from -2 to 2
- w_project: bfloat16 [1024, 256], replicated, may hold values from -0.1875 to 0.1875
- block_qkv: bfloat16 [256, 768], replicated, may hold values from -0.375 to 0.375
- block_out: bfloat16 [256, 256], replicated, may hold values from -0.375 to 0.375
- block_bias: float32 [8, 64, 64], replicated, may hold values from -3 to 250, as said below
- grid_qkv: bfloat16 [256, 768], replicated, may hold values from -0.375 to 0.375
- grid_out: bfloat16 [256, 256], replicated, may hold values from -0.375 to 0.375
- grid_bias: float32 [8, 64, 64], replicated, may hold values from -3 to 250, as said below
Outputs:
- result: bfloat16 [1024, 512, 256], P('row', 'col')
Inputs may be any that keep to these rules, and one draw needn't show every extreme that they name: `block_bias`: A learned bias for each head and each pair of query and key positions of a group. `grid_bias`: A learned bias for each head and each pair of query and key positions of a group.
All inputs are finite; a program needn't handle non-finite values.
Results may differ from a plain program's by a relative error of at most 0.012.
Values may be sent and summed in bfloat16 or wider, within the bound.
A program may use at most 128 MiB of HBM per device.

v0:
```python
import jax
import jax.numpy as jnp
from jax import lax
from jax.sharding import PartitionSpec as P

HEAD_DIM = 32
WINDOW = 8


def padded_2(x, sides, width):
    for axis, dim in sides:
        size, length = (lax.axis_size(axis), x.shape[dim])
        up = [(i, (i + 1) % size) for i in range(size - 1)]
        down = [(j, i) for i, j in up]
        last = lax.slice_in_dim(x, length - width, length, axis=dim)
        initial = lax.slice_in_dim(x, 0, width, axis=dim)
        before = lax.ppermute(last, axis, up)
        after = lax.ppermute(initial, axis, down)
        x = jnp.concatenate([before, x, after], axis=dim)
    return x


def layer_norm(values):
    values = values.astype(jnp.float32)
    centered = values - jnp.mean(values, axis=-1, keepdims=True)
    spread = jnp.mean(centered * centered, axis=-1, keepdims=True)
    return centered * lax.rsqrt(spread + 1e-05)


def expand_rows(values, w_expand):
    shape = values.shape
    normed = layer_norm(values).astype(jnp.bfloat16).reshape(-1, shape[-1])
    hidden = jax.nn.gelu(
        jnp.dot(normed, w_expand, preferred_element_type=jnp.float32), approximate=False
    )
    return hidden.astype(jnp.bfloat16).reshape(shape[:-1] + (w_expand.shape[1],))


def depthwise(padded, kernel, rows, cols):
    total = jnp.zeros((rows, cols, kernel.shape[2]), jnp.float32)
    for down in range(3):
        for across in range(3):
            total = total + padded[down : down + rows, across : across + cols].astype(
                jnp.float32
            ) * kernel[down, across].astype(jnp.float32)
    return total


def attend(tokens, w_qkv, w_out, bias):
    count, span, width = tokens.shape
    heads = width // HEAD_DIM
    normed = layer_norm(tokens).astype(jnp.bfloat16).reshape(-1, width)
    packed = jnp.dot(normed, w_qkv, preferred_element_type=jnp.float32).astype(jnp.bfloat16)
    packed = packed.reshape(count, span, 3, heads, HEAD_DIM)
    scores = jnp.einsum(
        "gqhd,gkhd->ghqk", packed[:, :, 0], packed[:, :, 1], preferred_element_type=jnp.float32
    )
    scores = scores / jnp.sqrt(jnp.float32(HEAD_DIM)) + bias[None]
    weights = jax.nn.softmax(scores, axis=-1).astype(jnp.bfloat16)
    mixed = jnp.einsum(
        "ghqk,gkhd->gqhd", weights, packed[:, :, 2], preferred_element_type=jnp.float32
    ).astype(jnp.bfloat16)
    mixed = mixed.reshape(count * span, width)
    output = tokens.reshape(-1, width).astype(jnp.float32) + jnp.dot(
        mixed, w_out, preferred_element_type=jnp.float32
    )
    return output.astype(jnp.bfloat16).reshape(count, span, width)


def on_device(
    image,
    w_expand,
    depth_kernel,
    w_project,
    block_qkv,
    block_out,
    block_bias,
    grid_qkv,
    grid_out,
    grid_bias,
):
    rows, cols, width = image.shape
    hidden = padded_2(expand_rows(image, w_expand), (("row", 0), ("col", 1)), 1)
    activated = jax.nn.gelu(depthwise(hidden, depth_kernel, rows, cols), approximate=False).astype(
        jnp.bfloat16
    )
    update = jnp.dot(
        activated.reshape(-1, activated.shape[2]), w_project, preferred_element_type=jnp.float32
    )
    first = (
        (image.reshape(-1, width).astype(jnp.float32) + update)
        .astype(jnp.bfloat16)
        .reshape(rows, cols, width)
    )
    windows = first.reshape(rows // WINDOW, WINDOW, cols // WINDOW, WINDOW, width).transpose(
        0, 2, 1, 3, 4
    )
    windows = windows.reshape(-1, WINDOW * WINDOW, width)
    second = attend(windows, block_qkv, block_out, block_bias)
    second = (
        second.reshape(rows // WINDOW, cols // WINDOW, WINDOW, WINDOW, width)
        .transpose(0, 2, 1, 3, 4)
        .reshape(rows, cols, width)
    )
    row_count = lax.axis_size("row")
    col_count = lax.axis_size("col")
    per_row = rows // row_count
    local_grid = WINDOW // col_count
    stride_c = cols // local_grid
    per_col = stride_c // col_count
    row_phase = row_count // WINDOW
    shaped = second.reshape(row_count, per_row, local_grid, col_count, per_col, width).transpose(
        0, 3, 1, 2, 4, 5
    )
    shaped = shaped.reshape(1, row_count * col_count, per_row, local_grid, per_col, width)
    moved = lax.all_to_all(shaped, ("row", "col"), split_axis=1, concat_axis=0, tiled=True)
    moved = moved.reshape(row_count, col_count, per_row, local_grid, per_col, width).transpose(
        0, 2, 1, 3, 4, 5
    )
    grouped = moved.reshape(
        WINDOW, row_phase, per_row, col_count, local_grid, per_col, width
    ).transpose(1, 2, 5, 0, 3, 4, 6)
    grouped = grouped.reshape(-1, WINDOW * WINDOW, width)
    done = attend(grouped, grid_qkv, grid_out, grid_bias)
    back = done.reshape(
        row_phase, per_row, per_col, WINDOW, col_count, local_grid, width
    ).transpose(3, 0, 1, 4, 5, 2, 6)
    back = back.reshape(row_count, per_row, col_count, local_grid, per_col, width)
    sending = back.transpose(0, 2, 1, 3, 4, 5).reshape(
        row_count * col_count, 1, per_row, local_grid, per_col, width
    )
    placed = lax.all_to_all(sending, ("row", "col"), split_axis=0, concat_axis=1, tiled=True)
    placed = placed.reshape(row_count, col_count, per_row, local_grid, per_col, width).transpose(
        0, 2, 3, 1, 4, 5
    )
    return placed.reshape(rows, cols, width)


def solution(mesh):
    in_specs = (P("row", "col", None), P(), P(), P(), P(), P(), P(), P(), P(), P())
    out_specs = P("row", "col", None)
    return jax.shard_map(
        on_device, mesh=mesh, in_specs=in_specs, out_specs=out_specs, check_vma=False
    )
```

profile of v0, /device:TPU:1, one launch (start us, length us, event | category | flops | bytes accessed | tf_op | source)
XLA Modules:
  0.0 510.0 jit_solution(8051950850950138138)
XLA Ops:
  0.0 2.3 convert_reduce_fusion
  2.3 2.5 multiply_reduce_fusion.2
  4.8 2.5 multiply_convert_fusion.1
  7.4 38.6 %fusion.4 = bf16[4096,1024]{1,0:T(8,128)(2,1)S(1)} fusion(bf16[4096,256]{1,0:T(8,128)(2,1)S(1)} %bitcast.132, bf16[256,1024]{1,0:T(8,128)(2,1)S(1)} %copy-done), kind=kOutput, calls=%fused_computation.6 | convolution fusion | flops 2420113408 | bytes 11010048 | tf_op jit(solution)/shard_map/dot_general | solution.py:34
  46.0 4.4 collective-permute-start
  50.4 1.3 collective-permute-start.1
  51.7 3.6 collective-permute-done
  55.4 4.2 collective-permute-done.1
  59.5 0.2 pad_maximum_fusion.5
  59.8 4.8 collective-permute-start.2
  64.6 2.1 collective-permute-start.3
  66.8 0.1 copy.102
  66.9 4.0 collective-permute-done.3
  70.9 18.6 %maximum_maximum_fusion = (bf16[34,129,1024]{2,1,0:T(8,128)(2,1)}, bf16[34,129,1024]{2,1,0:T(8,128)(2,1)}) fusion(bf16[1,128,1024]{2,1,0:T(8,128)(2,1)S(1)} %collective-permute-done.1, bf16[32,128,1024]{2,1,0:T(8,128)(2,1)} %bitcast.117, bf16[1,128,1024]{2,1,0:T(8,128)(2,1)S(1)} %collective-permute-done, bf16[34,1,1024]{2,1,0:T(2,128)(2,1)S(1)} %collective-permute-done.2, ...), kind=kLoop, calls=%fused_computation.49 | loop fusion | flops 71860224 | bytes 27017216 | tf_op jit(solution)/shard_map/concatenate | solution.py:19
  89.6 64.5 %fusion.7 = bf16[32,128,1024]{2,1,0:T(8,128)(2,1)} fusion(bf16[32,128,1024]{2,1,0:T(8,128)(2,1)} %bitcast.118, bf16[34,129,1024]{2,1,0:T(8,128)(2,1)} %get-tuple-element.12, bf16[1,128,1024]{2,1,0:T(8,128)(2,1)S(1)} %collective-permute-done.1, bf16[34,129,1024]{2,1,0:T(8,128)(2,1)} %get-tuple-element.11, bf16[1,128,1024]{2,1,0:T(8,128)(2,1)S(1)} %collective-permute-done, ...), kind=kLoop, calls=%fused_computation.9 | loop fusion | flops 390070272 | bytes 67670016 | tf_op jit(solution)/shard_map/convert_element_type | solution.py:84
  154.1 5.9 %fusion.32 = bf16[4096,256]{1,0:T(8,128)(2,1)S(1)} fusion(bf16[4096,1024]{1,0:T(8,128)(2,1)} %bitcast.131, bf16[1024,256]{1,0:T(8,128)(2,1)S(1)} %copy-done.11, bf16[4096,256]{1,0:T(8,128)(2,1)S(1)} %bitcast.125), kind=kOutput, calls=%fused_computation.66 | convolution fusion | flops 2150629376 | bytes 13107200 | tf_op jit(solution)/shard_map/dot_general | solution.py:87
  159.9 2.4 convert_bitcast_fusion.1
  162.4 0.6 fusion.37
  163.1 0.1 copy.95
  163.3 0.1 copy.94
  163.4 1.3 multiply_reduce_fusion.1
  164.9 0.1 copy.97
  165.1 0.1 rsqrt.32
  165.2 4.9 copy.92
  170.1 0.1 div.47
  170.2 3.3 fusion.36
  173.6 5.5 %convolution_convert_fusion.1 = bf16[4096,768]{1,0:T(8,128)(2,1)} fusion(bf16[4096,256]{1,0:T(8,128)(2,1)S(1)} %fusion.36, bf16[256,768]{1,0:T(8,128)(2,1)} %param.14), kind=kOutput, calls=%fused_computation.60 | convolution fusion | flops 1613758464 | bytes 8781824 | tf_op jit(solution)/shard_map/dot_general | solution.py:53
  179.1 8.6 %copy.98 = bf16[4096,768]{0,1:T(8,128)(2,1)} copy(bf16[4096,768]{1,0:T(8,128)(2,1)} %convolution_convert_fusion.1) | data formatting | bytes 12582912 | tf_op jit(solution)/shard_map/convert_element_type | solution.py:53
  187.7 17.9 %reshape.154 = bf16[64,64,3,8,32]{1,0,4,3,2:T(8,128)(2,1)} reshape(bf16[4096,768]{0,1:T(8,128)(2,1)} %copy.98) | data formatting | bytes 12582912 | tf_op jit(solution)/shard_map/reshape | solution.py:54
  205.6 7.5 %fusion.46 = (bf16[64,64,1,8,32]{1,0,4,3,2:T(8,128)(2,1)}, bf16[64,64,1,8,32]{1,0,4,3,2:T(8,128)(2,1)S(1)}, bf16[64,64,1,8,32]{1,0,4,3,2:T(8,128)(2,1)S(1)}) fusion(bf16[64,64,3,8,32]{1,0,4,3,2:T(8,128)(2,1)} %reshape.154), kind=kLoop, calls=%fused_computation.117 | loop fusion | bytes 12582912 | tf_op jit(solution)/shard_map/slice | solution.py:61
  213.1 21.2 %fusion.34 = f32[64,8,64,64]{2,3,1,0:T(8,128)} fusion(bf16[64,64,1,8,32]{1,0,4,3,2:T(8,128)(2,1)S(1)} %get-tuple-element.10, bf16[64,64,1,8,32]{1,0,4,3,2:T(8,128)(2,1)S(1)} %get-tuple-element.9), kind=kOutput, calls=%fused_computation.72 | convolution fusion | flops 134217728 | bytes 12582912 | tf_op jit(solution)/shard_map/gqhd,gkhd->ghqk/dot_general | solution.py:55
  234.3 17.7 %fusion.47 = (f32[64,8,64]{2,1,0:T(8,128)S(1)}, f32[64,8,64,64]{2,3,1,0:T(8,128)}) fusion(f32[64,8,64,64]{2,3,1,0:T(8,128)} %fusion.34, f32[8,64,64]{1,2,0:T(8,128)S(1)} %copy.102), kind=kOutput, calls=%fused_computation.118 | output fusion | flops 12582975 | bytes 17039360 | tf_op jit(solution)/shard_map/sub | solution.py:59
  252.0 18.0 %convert_bitcast_fusion.3 = bf16[64,64,8,32]{1,3,2,0:T(8,128)(2,1)} fusion(f32[64,8,64,64]{2,3,1,0:T(8,128)} %get-tuple-element.27, f32[64,8,64]{2,1,0:T(8,128)S(1)} %get-tuple-element.26, bf16[64,64,1,8,32]{1,0,4,3,2:T(8,128)(2,1)} %get-tuple-element.8), kind=kOutput, calls=%fused_computation.83 | convolution fusion | flops 139460608 | bytes 12713984 | tf_op jit(solution)/shard_map/ghqk,gkhd->gqhd/dot_general | solution.py:60
  270.1 7.3 %copy.104 = bf16[64,64,8,32]{1,0,3,2:T(8,128)(2,1)} copy(bf16[64,64,8,32]{1,3,2,0:T(8,128)(2,1)} %convert_bitcast_fusion.3) | data formatting | bytes 4194304 | tf_op jit(solution)/shard_map/convert_element_type | solution.py:62
  277.4 5.7 %reshape.155 = bf16[4096,256]{0,1:T(8,128)(2,1)S(1)} reshape(bf16[64,64,8,32]{1,0,3,2:T(8,128)(2,1)} %copy.104) | data formatting | bytes 4194304 | tf_op jit(solution)/shard_map/reshape | solution.py:63
  283.1 3.0 fusion.30
  286.0 0.3 copy.105
  286.3 1.6 copy.106
  287.9 12.7 %all-to-all-start = ((bf16[1,128,1,2,16,256]{5,4,3,2,0,1:T(8,128)(2,1)}), bf16[1,128,1,2,16,256]{5,4,3,2,0,1:T(8,128)(2,1)S(1)}, u32[]{:S(2)}, u32[]{:S(2)}) async-start(bf16[1,128,1,2,16,256]{5,4,3,2,0,1:T(8,128)(2,1)} %bitcast.126), calls=%async_computation | async-start | bytes 4194304 | tf_op jit(solution)/shard_map/all_to_all | solution.py:116
  300.6 0.1 copy.119
  300.8 29.9 %all-to-all-done = bf16[1,128,1,2,16,256]{5,4,3,2,0,1:T(8,128)(2,1)S(1)} async-done(((bf16[1,128,1,2,16,256]{5,4,3,2,0,1:T(8,128)(2,1)}), bf16[1,128,1,2,16,256]{5,4,3,2,0,1:T(8,128)(2,1)S(1)}, u32[]{:S(2)}, u32[]{:S(2)}) %all-to-all-start) | async-done | bytes 2097184 | tf_op jit(solution)/shard_map/all_to_all | solution.py:116
  330.6 0.8 fusion.38
  331.5 2.6 convert_bitcast_fusion
  334.2 1.9 copy.111
  336.1 1.4 multiply_reduce_fusion
  337.6 1.2 copy.114
  338.8 0.9 rsqrt.34
  339.7 7.4 %copy.109 = f32[4,1,16,8,4,2,256]{6,5,4,3,2,0,1:T(2,128)} copy(f32[4,1,16,8,4,2,256]{6,2,5,4,0,3,1:T(8,128)} %convert_bitcast_fusion) | data formatting | bytes 8388608 | tf_op jit(solution)/shard_map/convert_element_type | solution.py:64
  347.0 6.1 %reshape.172 = f32[4096,256]{1,0:T(8,128)} reshape(f32[4,1,16,8,4,2,256]{6,5,4,3,2,0,1:T(2,128)} %copy.109) | data formatting | bytes 8388608 | tf_op jit(solution)/shard_map/convert_element_type | solution.py:64
  353.1 0.9 div.53
  354.0 5.9 %convolution_convert_fusion = bf16[4096,768]{1,0:T(8,128)(2,1)} fusion(bf16[256,768]{1,0:T(8,128)(2,1)S(1)} %copy-done.5, f32[4096,256]{1,0:T(8,128)} %reshape.172, f32[4096]{0:T(1024)S(1)} %rsqrt.34, f32[4096]{0:T(1024)S(1)} %div.53), kind=kOutput, calls=%fused_computation.59 | convolution fusion | flops 1616904192 | bytes 10911744 | tf_op jit(solution)/shard_map/dot_general | solution.py:53
  359.9 8.6 %copy.115 = bf16[4096,768]{0,1:T(8,128)(2,1)} copy(bf16[4096,768]{1,0:T(8,128)(2,1)} %convolution_convert_fusion) | data formatting | bytes 12582912 | tf_op jit(solution)/shard_map/convert_element_type | solution.py:53
  368.5 17.9 %reshape.157 = bf16[64,64,3,8,32]{1,0,4,3,2:T(8,128)(2,1)} reshape(bf16[4096,768]{0,1:T(8,128)(2,1)} %copy.115) | data formatting | bytes 12582912 | tf_op jit(solution)/shard_map/reshape | solution.py:54
  386.4 7.7 %fusion.45 = (bf16[64,64,1,8,32]{1,0,4,3,2:T(8,128)(2,1)}, bf16[64,64,1,8,32]{1,0,4,3,2:T(8,128)(2,1)S(1)}, bf16[64,64,1,8,32]{1,0,4,3,2:T(8,128)(2,1)S(1)}) fusion(bf16[64,64,3,8,32]{1,0,4,3,2:T(8,128)(2,1)} %reshape.157), kind=kLoop, calls=%fused_computation.116 | loop fusion | bytes 12582912 | tf_op jit(solution)/shard_map/slice | solution.py:61
  394.1 21.2 %fusion.33 = f32[64,8,64,64]{2,3,1,0:T(8,128)} fusion(bf16[64,64,1,8,32]{1,0,4,3,2:T(8,128)(2,1)S(1)} %get-tuple-element.7, bf16[64,64,1,8,32]{1,0,4,3,2:T(8,128)(2,1)S(1)} %get-tuple-element.6), kind=kOutput, calls=%fused_computation.68 | convolution fusion | flops 134217728 | bytes 12582912 | tf_op jit(solution)/shard_map/gqhd,gkhd->ghqk/dot_general | solution.py:55
  415.3 17.8 %fusion.48 = (f32[64,8,64]{2,1,0:T(8,128)S(1)}, f32[64,8,64,64]{2,3,1,0:T(8,128)}) fusion(f32[64,8,64,64]{2,3,1,0:T(8,128)} %fusion.33, f32[8,64,64]{1,2,0:T(8,128)S(1)} %copy.119), kind=kOutput, calls=%fused_computation.119 | output fusion | flops 12582975 | bytes 17039360 | tf_op jit(solution)/shard_map/sub | solution.py:59
  433.1 18.0 %convert_bitcast_fusion.2 = bf16[64,64,8,32]{1,3,2,0:T(8,128)(2,1)} fusion(f32[64,8,64,64]{2,3,1,0:T(8,128)} %get-tuple-element.29, f32[64,8,64]{2,1,0:T(8,128)S(1)} %get-tuple-element.28, bf16[64,64,1,8,32]{1,0,4,3,2:T(8,128)(2,1)} %get-tuple-element.5), kind=kOutput, calls=%fused_computation.80 | convolution fusion | flops 139460608 | bytes 12713984 | tf_op jit(solution)/shard_map/ghqk,gkhd->gqhd/dot_general | solution.py:60
  451.1 7.2 %copy.121 = bf16[64,64,8,32]{1,0,3,2:T(8,128)(2,1)} copy(bf16[64,64,8,32]{1,3,2,0:T(8,128)(2,1)} %convert_bitcast_fusion.2) | data formatting | bytes 4194304 | tf_op jit(solution)/shard_map/convert_element_type | solution.py:62
  458.3 5.7 %reshape.158 = bf16[4096,256]{0,1:T(8,128)(2,1)S(1)} reshape(bf16[64,64,8,32]{1,0,3,2:T(8,128)(2,1)} %copy.121) | data formatting | bytes 4194304 | tf_op jit(solution)/shard_map/reshape | solution.py:63
  464.0 4.3 fusion.31
  468.3 2.7 reshape_reshape.14
  471.0 2.3 copy.122
  473.3 34.6 %all_to_all.8 = bf16[128,1,1,2,16,256]{5,4,3,2,1,0:T(8,128)(2,1)S(1)} all-to-all(bf16[128,1,1,2,16,256]{5,4,3,2,1,0:T(8,128)(2,1)S(1)} %bitcast.128), channel_id=1, replica_groups=mesh['row'=32,'col'=4] {'row','col'}, dimensions={0} | all-to-all | bytes 4194304 | tf_op jit(solution)/shard_map/all_to_all | solution.py:132
  507.9 1.6 copy.124
  (36 shorter events, 0.7 us)
Async XLA Ops:
  0.0 7.3 %copy-start = (bf16[256,1024]{1,0:T(8,128)(2,1)S(1)}, bf16[256,1024]{1,0:T(8,128)(2,1)}, u32[]{:S(2)}) copy-start(bf16[256,1024]{1,0:T(8,128)(2,1)} %param.11) | copy-start | bytes 1572868
  7.3 59.4 %copy-start.10 = (bf16[3,3,1024]{2,1,0:T(4,128)(2,1)S(1)}, bf16[3,3,1024]{2,1,0:T(4,128)(2,1)}, u32[]{:S(2)}) copy-start(bf16[3,3,1024]{2,1,0:T(4,128)(2,1)} %param.12) | copy-start | bytes 55300
  7.4 59.4 %copy-start.6 = (f32[8,64,64]{2,1,0:T(8,128)S(1)}, f32[8,64,64]{2,1,0:T(8,128)}, u32[]{:S(2)}) copy-start(f32[8,64,64]{2,1,0:T(8,128)} %param.16) | copy-start | bytes 393220
  46.0 13.6 %copy-start.2 = (bf16[4096,1024]{1,0:T(8,128)(2,1)}, bf16[4096,1024]{1,0:T(8,128)(2,1)S(1)}, u32[]{:S(2)}) copy-start(bf16[4096,1024]{1,0:T(8,128)(2,1)S(1)} %fusion.4) | copy-start | bytes 25165828
  46.0 9.3 %collective-permute-start = (bf16[1,128,1024]{2,1,0:T(8,128)(2,1)S(1)}, bf16[1,128,1024]{2,1,0:T(8,128)(2,1)S(1)}, u32[]{:S(2)}, u32[]{:S(2)}) collective-permute-start(bf16[1,128,1024]{2,1,0:T(8,128)(2,1)S(1)} %get-tuple-element.15), channel_id=1, source_target_pairs={{0,4},{4,8},{8,12},{12,16},{16,20},{20,24},{24,28},{28,32},{32,36}... | collective-permute-start | bytes 786440 | tf_op jit(solution)/shard_map/ppermute | solution.py:17
  50.4 9.1 %collective-permute-start.1 = (bf16[1,128,1024]{2,1,0:T(8,128)(2,1)S(1)}, bf16[1,128,1024]{2,1,0:T(8,128)(2,1)S(1)}, u32[]{:S(2)}, u32[]{:S(2)}) collective-permute-start(bf16[1,128,1024]{2,1,0:T(8,128)(2,1)S(1)} %get-tuple-element.16), channel_id=1, source_target_pairs={{4,0},{8,4},{12,8},{16,12},{20,16},{24,20},{28,24},{32,28},{36,32}... | collective-permute-start | bytes 786440 | tf_op jit(solution)/shard_map/ppermute | solution.py:18
  59.8 7.1 %collective-permute-start.2 = (bf16[34,1,1024]{2,1,0:T(2,128)(2,1)S(1)}, bf16[34,1,1024]{2,1,0:T(2,128)(2,1)S(1)}, u32[]{:S(2)}, u32[]{:S(2)}) collective-permute-start(bf16[34,1,1024]{2,1,0:T(2,128)(2,1)S(1)} %get-tuple-element.13), channel_id=1, source_target_pairs={{0,1},{1,2},{2,3},{4,5},{5,6},{6,7},{8,9},{9,10},{10,11},{12,13},{... | collective-permute-start | bytes 208904 | tf_op jit(solution)/shard_map/ppermute | solution.py:17
  64.6 6.4 %collective-permute-start.3 = (bf16[34,1,1024]{2,1,0:T(2,128)(2,1)S(1)}, bf16[34,1,1024]{2,1,0:T(2,128)(2,1)S(1)}, u32[]{:S(2)}, u32[]{:S(2)}) collective-permute-start(bf16[34,1,1024]{2,1,0:T(2,128)(2,1)S(1)} %get-tuple-element.14), channel_id=1, source_target_pairs={{1,0},{2,1},{3,2},{5,4},{6,5},{7,6},{9,8},{10,9},{11,10},{13,12},{... | collective-permute-start | bytes 208904 | tf_op jit(solution)/shard_map/ppermute | solution.py:18
  89.6 64.5 %copy-start.3 = (bf16[32,128,256]{2,1,0:T(8,128)(2,1)S(1)}, bf16[32,128,256]{2,1,0:T(8,128)(2,1)}, u32[]{:S(2)}) copy-start(bf16[32,128,256]{2,1,0:T(8,128)(2,1)} %param.10) | copy-start | bytes 6291460
  89.6 64.5 %copy-start.11 = (bf16[1024,256]{1,0:T(8,128)(2,1)S(1)}, bf16[1024,256]{1,0:T(8,128)(2,1)}, u32[]{:S(2)}) copy-start(bf16[1024,256]{1,0:T(8,128)(2,1)} %param.13) | copy-start | bytes 1572868
  252.0 31.0 %copy-start.8 = (bf16[256,256]{1,0:T(8,128)(2,1)S(1)}, bf16[256,256]{1,0:T(8,128)(2,1)}, u32[]{:S(2)}) copy-start(bf16[256,256]{1,0:T(8,128)(2,1)} %param.15) | copy-start | bytes 393220
  270.1 30.5 %copy-start.7 = (f32[8,64,64]{2,1,0:T(8,128)S(1)}, f32[8,64,64]{2,1,0:T(8,128)}, u32[]{:S(2)}) copy-start(f32[8,64,64]{2,1,0:T(8,128)} %param.19) | copy-start | bytes 393220
  287.9 42.8 %all-to-all-start = ((bf16[1,128,1,2,16,256]{5,4,3,2,0,1:T(8,128)(2,1)}), bf16[1,128,1,2,16,256]{5,4,3,2,0,1:T(8,128)(2,1)S(1)}, u32[]{:S(2)}, u32[]{:S(2)}) async-start(bf16[1,128,1,2,16,256]{5,4,3,2,0,1:T(8,128)(2,1)} %bitcast.126), calls=%async_computation | async-start | bytes 4194304 | tf_op jit(solution)/shard_map/all_to_all | solution.py:116
  300.6 53.4 %copy-start.5 = (bf16[256,768]{1,0:T(8,128)(2,1)S(1)}, bf16[256,768]{1,0:T(8,128)(2,1)}, u32[]{:S(2)}) copy-start(bf16[256,768]{1,0:T(8,128)(2,1)} %param.17) | copy-start | bytes 1179652
  337.5 15.6 %copy-start.4 = (f32[4,16,8,4,2]{4,3,2,1,0:T(4,128)S(1)}, f32[4,16,8,4,2]{4,3,2,1,0:T(4,128)}, u32[]{:S(2)}) copy-start(f32[4,16,8,4,2]{4,3,2,1,0:T(4,128)} %copy.111) | copy-start | bytes 49156
  433.1 30.9 %copy-start.9 = (bf16[256,256]{1,0:T(8,128)(2,1)S(1)}, bf16[256,256]{1,0:T(8,128)(2,1)}, u32[]{:S(2)}) copy-start(bf16[256,256]{1,0:T(8,128)(2,1)} %param.18) | copy-start | bytes 393220
  451.1 58.4 %copy-start.1 = (bf16[256,1024]{1,0:T(8,128)(2,1)S(1)}, bf16[256,1024]{1,0:T(8,128)(2,1)}, u32[]{:S(2)}) copy-start(bf16[256,1024]{1,0:T(8,128)(2,1)} %param.11) | copy-start | bytes 1572868
where the time goes:
time: 516 us; the launch traced here: 510 us
  matrix products  142 us (28%)
  other arithmetic  139 us (27%)
  local copies, waits for them, and re-layouts  127 us (25%)
  waiting for transfers between devices  41.7 us (8%)
  blocking collectives  34.6 us (7%)
  starting transfers between devices  25.3 us (5%)
    convert_element_type x1, other arithmetic, on_device(): jax.nn.gelu(depthwise(hidden, depth_kernel, rows, cols), approximate=False)  64.5 us
    dot_general x2, matrix products, attend(): jnp.einsum('gqhd,gkhd->ghqk', packed[:, :, 0], packed[:, :, 1], preferred...  42.4 us
    dot_general x1, matrix products, expand_rows(): jnp.dot(normed, w_expand, preferred_element_type=jnp.float32)  38.6 us
    dot_general x2, matrix products, attend(): jnp.einsum('ghqk,gkhd->gqhd', weights, packed[:, :, 2], preferred_element...  36.1 us
    reshape x2, local copies, waits for them, and re-layouts, attend(): packed = packed.reshape(count, span, 3, heads, HEAD_DIM)  35.8 us
    sub x2, other arithmetic, attend(): weights = jax.nn.softmax(scores, axis=-1).astype(jnp.bfloat16)  35.5 us
    all_to_all x1, blocking collectives, on_device(): lax.all_to_all(sending, ('row', 'col'), split_axis=0, concat_axis=1, tile...  34.6 us
    all_to_all x1, waiting for transfers between devices, on_device(): lax.all_to_all(shaped, ('row', 'col'), split_axis=1, concat_axis=0, tiled...  29.9 us
  transfers between devices with their start and end apart: 5, of which 4 were waited for; matrix products, arithmetic and copies ran while one was open for 0% of the time, Pallas kernels for 0%

commit v1 on v0

v1 whole, which is shorter than its diff:
```python
import functools

import jax
import jax.numpy as jnp
from jax import lax
from jax.experimental import pallas as pl
from jax.experimental.pallas import tpu as pltpu
from jax.sharding import PartitionSpec as P

MESH = pl.DeviceIdType.MESH
HEADS = 8
HEAD_DIM = 32
WIDTH = 256
EXPANDED = 1024
LOG2E = 1.4426950408889634
ROOT2 = 1.4142135623730951
BF = jnp.bfloat16
F32 = jnp.float32


def dot(a, b):
    return jnp.dot(a, b, preferred_element_type=F32)


def dot_nt(a, b):
    return lax.dot_general(a, b, (((1,), (1,)), ((), ())), preferred_element_type=F32)


def layer_norm(v):
    mean = jnp.mean(v, axis=-1, keepdims=True)
    cen = v - mean
    var = jnp.mean(cen * cen, axis=-1, keepdims=True)
    return cen * lax.rsqrt(var + 1e-5)


def gelu_of_half(z):
    return z + z * lax.erf(z * jnp.asarray(ROOT2, z.dtype))


def perm_image():
    out = lax.broadcasted_iota(jnp.int32, (256, 256), 0)
    src = lax.broadcasted_iota(jnp.int32, (256, 256), 1)
    want = (out & 128) | ((out & 15) << 3) | ((out >> 4) & 7)
    return (src == want).astype(F32).astype(BF)


def perm_image_back():
    out = lax.broadcasted_iota(jnp.int32, (256, 256), 0)
    src = lax.broadcasted_iota(jnp.int32, (256, 256), 1)
    want = (out & 128) | ((out & 7) << 4) | ((out >> 3) & 15)
    return (src == want).astype(F32).astype(BF)


def perm_swap():
    out = lax.broadcasted_iota(jnp.int32, (256, 256), 0)
    src = lax.broadcasted_iota(jnp.int32, (256, 256), 1)
    want = ((out & 15) << 4) | (out >> 4)
    return (src == want).astype(F32).astype(BF)


def perm_grid():
    out = lax.broadcasted_iota(jnp.int32, (256, 256), 0)
    src = lax.broadcasted_iota(jnp.int32, (256, 256), 1)
    group, pos = out >> 4, out & 15
    j0, s = group >> 3, group & 7
    want = ((pos >> 1) << 5) | (j0 << 4) | ((pos & 1) << 3) | s
    return (src == want).astype(F32).astype(BF)


def perm_grid_back():
    out = lax.broadcasted_iota(jnp.int32, (256, 256), 0)
    src = lax.broadcasted_iota(jnp.int32, (256, 256), 1)
    msg, j0, jl, s = out >> 5, (out >> 4) & 1, (out >> 3) & 1, out & 7
    want = (((j0 << 3) | s) << 4) | (msg << 1) | jl
    return (src == want).astype(F32).astype(BF)


def spread(x, masks, zero):
    parts = []
    for t in range(4):
        lo, hi = x[16 * t : 16 * t + 16, :128], x[16 * t : 16 * t + 16, 128:]
        for h in range(4):
            parts.append(jnp.concatenate([lo * masks[h], zero], axis=1))
        for h in range(4):
            parts.append(jnp.concatenate([zero, hi * masks[h]], axis=1))
    return jnp.concatenate(parts, axis=0)


def attention(tok, res, w_qkv, w_out, bias, ones):
    lane = lax.broadcasted_iota(jnp.int32, (64, 128), 1)
    mlane = lax.broadcasted_iota(jnp.int32, (16, 128), 1)
    masks = [(mlane // HEAD_DIM == h).astype(F32).astype(BF) for h in range(4)]
    zero = jnp.zeros((16, 128), BF)

    def step(c, carry):
        t = tok[pl.ds(4 * c, 4)].reshape(256, WIDTH)
        normed = layer_norm(t).astype(BF)
        qkv = dot(normed, w_qkv[...])
        q = (qkv[:, :WIDTH] * (LOG2E / HEAD_DIM**0.5)).astype(BF)
        k = qkv[:, WIDTH : 2 * WIDTH].astype(BF)
        v = qkv[:, 2 * WIDTH :].astype(BF)
        mixed = []
        for g in range(4):
            rows = slice(64 * g, 64 * g + 64)
            z = dot_nt(q[rows], spread(k[rows], masks, zero)) + bias[...]
            tiles = [z[:, 128 * n : 128 * n + 128] for n in range(4)]
            m = jnp.maximum(jnp.maximum(tiles[0], tiles[1]), jnp.maximum(tiles[2], tiles[3]))
            for bit in (8, 4, 2, 1):
                m = jnp.maximum(m, jnp.take_along_axis(m, lane ^ bit, axis=1))
            p = jnp.concatenate([jnp.exp2(x - m).astype(BF) for x in tiles], axis=1)
            num = dot(p, spread(v[rows], masks, zero))
            den = dot(p, ones[...])
            mixed.append((num / den).astype(BF))
        out = dot(jnp.concatenate(mixed, axis=0), w_out[...]) + t
        res[pl.ds(4 * c, 4)] = out.astype(BF).reshape(4, 64, WIDTH)
        return carry

    lax.fori_loop(0, 4, step, 0)


def kernel(
    image, w_expand, depth, w_project, b_qkv, b_out, b_bias, g_qkv, g_out, g_bias,
    result,
    halo_tb, halo_l, halo_r, edge_l, edge_r, send1, recv1, send2, recv2,
    hidden, image_p, w_half, taps, hid_l, hid_r, act, tok, res, perms, ones,
    halo_send, halo_recv, send_sem1, recv_sem1, send_sem2, recv_sem2,
):
    R, C = lax.axis_index("row"), lax.axis_index("col")
    plane, mine = R % 4, (R // 4) * 4 + C

    def device(d):
        return {"row": (d // 4) * 4 + plane, "col": d % 4}

    up, down = (R + 31) % 32, (R + 1) % 32
    left, right = (C + 3) % 4, (C + 1) % 4

    barrier = pltpu.get_barrier_semaphore()

    def greet(n, carry):
        pl.semaphore_signal(barrier, inc=1, device_id=device((mine + n) % 32), device_id_type=MESH)
        return carry

    lax.fori_loop(1, 32, greet, 0)
    for r in (up, down):
        for c in (left, C, right):
            pl.semaphore_signal(barrier, inc=1, device_id={"row": r, "col": c}, device_id_type=MESH)

    perms[0] = perm_image()
    perms[1] = perm_image_back()
    perms[2] = perm_swap()
    perms[3] = perm_grid()
    perms[4] = perm_grid_back()
    row_head = (lax.broadcasted_iota(jnp.int32, (512, WIDTH), 0) // 16) % HEADS
    lane_head = lax.broadcasted_iota(jnp.int32, (512, WIDTH), 1) // HEAD_DIM
    ones[...] = (row_head == lane_head).astype(F32).astype(BF)
    w_half[...] = w_expand[...] * jnp.asarray(0.5, BF)
    for n in range(9):
        tap = depth[n // 3, pl.ds(n % 3, 1), :].astype(F32) * 0.5
        taps[n] = jnp.broadcast_to(tap, (16, EXPANDED)).astype(BF)
    row16 = lax.broadcasted_iota(jnp.int32, (32, 16, WIDTH), 1)
    edge_l[...] = jnp.sum(
        jnp.where(row16 == 0, image[:, 0:16, :].astype(F32), 0.0), axis=1
    ).astype(BF)
    edge_r[...] = jnp.sum(
        jnp.where(row16 == 15, image[:, 112:128, :].astype(F32), 0.0), axis=1
    ).astype(BF)

    def expand(tokens, row0, row1, keep):
        x = dot(perms[0], tokens)
        if keep is not None:
            image_p[keep] = x.astype(BF)
        normed = layer_norm(x).astype(BF)
        for n in range(4):
            ch = slice(256 * n, 256 * n + 256)
            h = gelu_of_half(dot(normed, w_half[:, ch])).astype(BF)
            hidden[row0, 1:9, :, ch] = h[:128].reshape(8, 16, 256)
            hidden[row1, 1:9, :, ch] = h[128:].reshape(8, 16, 256)

    def expand_image(b):
        rows = image[pl.ds(2 * b, 2)].reshape(256, WIDTH)
        expand(rows, 2 * b + 1, 2 * b + 2, b)

    expand_image(0)
    pl.semaphore_wait(barrier, 37)

    def halo_copies():
        plan = (
            (image.at[31], halo_tb.at[0], down, C),
            (image.at[0], halo_tb.at[1], up, C),
            (edge_r, halo_l.at[pl.ds(16, 32)], R, right),
            (edge_l, halo_r.at[pl.ds(16, 32)], R, left),
            (edge_r.at[pl.ds(16, 16)], halo_l.at[pl.ds(0, 16)], down, right),
            (edge_r.at[pl.ds(0, 16)], halo_l.at[pl.ds(48, 16)], up, right),
            (edge_l.at[pl.ds(16, 16)], halo_r.at[pl.ds(0, 16)], down, left),
            (edge_l.at[pl.ds(0, 16)], halo_r.at[pl.ds(48, 16)], up, left),
        )
        return [
            pltpu.make_async_remote_copy(
                src_ref=src, dst_ref=dst, send_sem=halo_send.at[n], recv_sem=halo_recv.at[n],
                device_id={"row": r, "col": c}, device_id_type=MESH,
            )
            for n, (src, dst, r, c) in enumerate(plan)
        ]

    halos = halo_copies()
    for copy in halos:
        copy.start()
    expand_image(1)
    for copy in halos:
        copy.wait()

    row64 = lax.broadcasted_iota(jnp.int32, (64, WIDTH), 0)
    off_grid = ((row64 <= 15) & (R == 0)) | ((row64 >= 48) & (R == 31))
    for halo, off, hid in ((halo_l, C == 0, hid_l), (halo_r, C == 3, hid_r)):
        x = jnp.where(off_grid | off, 0.0, halo[...].astype(F32))
        hid[...] = gelu_of_half(dot(layer_norm(x).astype(BF), w_half[...]))
    row256 = lax.broadcasted_iota(jnp.int32, (256, WIDTH), 0)
    off_grid = ((row256 < 128) & (R == 0)) | ((row256 >= 128) & (R == 31))
    x = jnp.where(off_grid, 0.0, halo_tb[...].reshape(256, WIDTH).astype(F32)).astype(BF)
    expand(x, 0, 33, None)

    row_s = lax.broadcasted_iota(jnp.int32, (16, EXPANDED), 0)

    def edges(r):
        from_left = pltpu.roll(hidden[r, 8].astype(F32), 1, 0)
        hidden[r, 0] = jnp.where(row_s == 0, hid_l[pl.ds(15 + r, 1), :], from_left).astype(BF)
        from_right = pltpu.roll(hidden[r, 1].astype(F32), 15, 0)
        hidden[r, 9] = jnp.where(row_s == 15, hid_r[pl.ds(15 + r, 1), :], from_right).astype(BF)

    for r in range(2):
        edges(r)

    def convolve(b):
        for row in range(2):
            for n in range(8):
                ch = slice(128 * n, 128 * n + 128)
                total = None
                for dr in range(3):
                    for dc in range(3):
                        term = hidden[2 * b + row + dr, dc : dc + 8, :, ch] * taps[3 * dr + dc, :, ch]
                        total = term if total is None else total + term
                act[128 * row : 128 * row + 128, ch] = gelu_of_half(total).reshape(128, 128)
        update = dot(act[...], w_project[...])
        return (image_p[b].astype(F32) + update).astype(BF)

    def exchange(src_of, dst_of, send_sem, recv_sem):
        own = pltpu.make_async_copy(src_of(mine), dst_of(mine), recv_sem)
        own.start()

        def send(n, carry):
            d = (mine + n) % 32
            pltpu.make_async_remote_copy(
                src_ref=src_of(d), dst_ref=dst_of(mine), send_sem=send_sem, recv_sem=recv_sem,
                device_id=device(d), device_id_type=MESH,
            ).start()
            return carry

        lax.fori_loop(1, 32, send, 0)

    def image_part(buf, k):
        return lambda d: buf.at[8 * k + d // 4, pl.ds(2 * (d % 4), 2)]

    def grid_part(buf, k):
        return lambda d: buf.at[k, d]

    def reorder_out(perm, store):
        for n in range(4):
            block = res[:, 16 * n : 16 * n + 16, :].reshape(256, WIDTH)
            store(n, dot(perm, block).astype(BF))

    def band(k, carry):
        @pl.when(k < 4)
        def _():
            def rows(n, carry):
                b = 4 * k + n

                @pl.when(b < 14)
                def _():
                    expand_image(b + 2)

                edges(2 * b + 2)
                edges(2 * b + 3)
                first = convolve(b)
                swapped = dot(perms[2], first).reshape(16, 16, WIDTH)
                tok[:, pl.ds(pl.multiple_of(16 * n, 16), 16), :] = swapped
                return carry

            lax.fori_loop(0, 4, rows, 0)
            attention(tok, res, b_qkv, b_out, b_bias, ones)

            def store(n, x):
                send1[pl.ds(8 * k + 2 * n, 2)] = x.reshape(2, 8, 16, WIDTH)

            reorder_out(perms[2], store)
            exchange(image_part(send1, k), grid_part(recv1, k), send_sem1.at[k], recv_sem1.at[k])

        @pl.when(k >= 1)
        def _():
            g = k - 1
            pltpu.make_async_copy(recv1.at[g], recv1.at[g], recv_sem1.at[g]).wait()
            for n in range(4):
                x = recv1[g, 8 * n : 8 * n + 8].reshape(256, WIDTH)
                tok[:, 16 * n : 16 * n + 16, :] = dot(perms[3], x).reshape(16, 16, WIDTH)
            attention(tok, res, g_qkv, g_out, g_bias, ones)

            def store(n, x):
                send2[g, 8 * n : 8 * n + 8] = x.reshape(8, 2, 16, WIDTH)

            reorder_out(perms[4], store)
            exchange_back(g)

        return carry

    def exchange_back(g):
        own = pltpu.make_async_copy(send2.at[g, mine], image_part(recv2, g)(mine), recv_sem2.at[g])
        own.start()

        def send(n, carry):
            d = (mine + n) % 32
            pltpu.make_async_remote_copy(
                src_ref=send2.at[g, d], dst_ref=image_part(recv2, g)(mine),
                send_sem=send_sem2.at[g], recv_sem=recv_sem2.at[g],
                device_id=device(d), device_id_type=MESH,
            ).start()
            return carry

        lax.fori_loop(1, 32, send, 0)

    lax.fori_loop(0, 5, band, 0)

    def finish(g, carry):
        view = recv2.at[pl.ds(8 * g, 8)]
        pltpu.make_async_copy(view, view, recv_sem2.at[g]).wait()
        for n in range(4):
            x = recv2[pl.ds(8 * g + 2 * n, 2)].reshape(256, WIDTH)
            result[pl.ds(8 * g + 2 * n, 2)] = dot(perms[1], x).astype(BF).reshape(2, 128, WIDTH)
        return carry

    lax.fori_loop(0, 4, finish, 0)

    def drain(g, carry):
        part = send2.at[g, pl.ds(0, 31)]
        pltpu.make_async_copy(part, part, send_sem1.at[g]).wait()
        pltpu.make_async_copy(part, part, send_sem2.at[g]).wait()
        return carry

    lax.fori_loop(0, 4, drain, 0)


def in_tiles(bias):
    tiled = (bias * LOG2E).reshape(HEADS, 64, 4, 16).transpose(1, 2, 0, 3)
    return tiled.reshape(64, 512)


def on_device(image, w_expand, depth, w_project, b_qkv, b_out, b_bias, g_qkv, g_out, g_bias):
    vmem = pl.BlockSpec(memory_space=pltpu.VMEM)
    dma = pltpu.SemaphoreType.DMA
    return pl.pallas_call(
        kernel,
        out_shape=jax.ShapeDtypeStruct(image.shape, BF),
        in_specs=[vmem] * 10,
        out_specs=vmem,
        scratch_shapes=[
            pltpu.VMEM((2, 128, WIDTH), BF),
            pltpu.VMEM((64, WIDTH), BF),
            pltpu.VMEM((64, WIDTH), BF),
            pltpu.VMEM((32, WIDTH), BF),
            pltpu.VMEM((32, WIDTH), BF),
            pltpu.VMEM((32, 8, 16, WIDTH), BF),
            pltpu.VMEM((4, 32, 2, 16, WIDTH), BF),
            pltpu.VMEM((4, 32, 2, 16, WIDTH), BF),
            pltpu.VMEM((32, 8, 16, WIDTH), BF),
            pltpu.VMEM((34, 10, 16, EXPANDED), BF),
            pltpu.VMEM((16, 256, WIDTH), BF),
            pltpu.VMEM((WIDTH, EXPANDED), BF),
            pltpu.VMEM((9, 16, EXPANDED), BF),
            pltpu.VMEM((64, EXPANDED), F32),
            pltpu.VMEM((64, EXPANDED), F32),
            pltpu.VMEM((256, EXPANDED), BF),
            pltpu.VMEM((16, 64, WIDTH), F32),
            pltpu.VMEM((16, 64, WIDTH), BF),
            pltpu.VMEM((5, 256, 256), BF),
            pltpu.VMEM((512, WIDTH), BF),
            dma((8,)),
            dma((8,)),
            dma((4,)),
            dma((4,)),
            dma((4,)),
            dma((4,)),
        ],
        compiler_params=pltpu.CompilerParams(
            collective_id=0, has_side_effects=True, vmem_limit_bytes=56 << 20
        ),
    )(
        image, w_expand, depth, w_project, b_qkv, b_out, in_tiles(b_bias),
        g_qkv, g_out, in_tiles(g_bias),
    )


def solution(mesh):
    in_specs = (P("row", "col", None),) + (P(),) * 9
    return jax.shard_map(
        on_device, mesh=mesh, in_specs=in_specs, out_specs=P("row", "col", None), check_vma=False
    )
```

time: 516 us -> 166 us (0.32); the launches traced: 510 us -> 166 us
  Pallas kernels: 0 us -> 160 us
  matrix products: 142 us -> 0 us
  other arithmetic: 139 us -> 0.05 us
  local copies, waits for them, and re-layouts: 127 us -> 5.98 us
  waiting for transfers between devices: 41.7 us -> 0 us
  blocking collectives: 34.6 us -> 0 us
  starting transfers between devices: 25.3 us -> 0 us
    pallas_call x0 -> x1, Pallas kernels: none -> 160 us  [on_device(): pl.pallas_call(kernel, out_shape=jax.ShapeDtypeStruct(image.shape, BF), i...]
    dot_general x10 -> x0, matrix products: 142 us -> none  [the longest x2 42.4 us: attend(): jnp.einsum('gqhd,gkhd->ghqk', packed[:, :, 0], packed[:, :, 1], preferred...]
    convert_element_type x5 -> x0, other arithmetic: 75.3 us -> none  [the longest x1 64.5 us: on_device(): jax.nn.gelu(depthwise(hidden, depth_kernel, rows, cols), approximate=False)]
    convert_element_type x7 -> x0, local copies, waits for them, and re-layouts: 50 us -> none  [the longest x3 18.3 us: attend(): tokens.reshape(-1, width).astype(jnp.float32)]
    reshape x4 -> x2, local copies, waits for them, and re-layouts: 47.1 us -> 1.56 us  [in_tiles(): return tiled.reshape(64, 512)]
    sub x2 -> x0, other arithmetic: 35.5 us -> none  [attend(): weights = jax.nn.softmax(scores, axis=-1).astype(jnp.bfloat16)]
    all_to_all x1 -> x0, blocking collectives: 34.6 us -> none  [on_device(): lax.all_to_all(sending, ('row', 'col'), split_axis=0, concat_axis=1, tile...]
    all_to_all x1 -> x0, waiting for transfers between devices: 29.9 us -> none  [on_device(): lax.all_to_all(shaped, ('row', 'col'), split_axis=1, concat_axis=0, tiled...]
  transfers between devices with their start and end apart: 5 -> 0, of which waited for: 4 -> 0; matrix products, arithmetic and copies ran while one was open for 0% -> 0% of each run, Pallas kernels for 0% -> 0%
where the time goes in v1:
time: 166 us
  Pallas kernels  160 us (96%)
  local copies, waits for them, and re-layouts  5.98 us (4%)
    pallas_call x1, Pallas kernels, on_device(): pl.pallas_call(kernel, out_shape=jax.ShapeDtypeStruct(image.shape, BF), i...  160 us
    unnamed x5, local copies, waits for them, and re-layouts  4.38 us

profile of v1, /device:TPU:1, one launch (start us, length us, event | category | flops | bytes accessed | tf_op | source)
XLA Modules:
  0.0 165.8 jit_solution(1305680241748030862)
XLA Ops:
  0.0 0.0 copy-start
  0.0 1.1 copy.13
  1.2 0.8 copy.17.b_bias
  2.0 0.0 copy-done
  2.0 0.1 copy.15
  2.2 0.8 copy.18.g_bias
  2.9 159.7 %shard_map.100 = bf16[32,128,256]{2,1,0:T(8,128)(2,1)} custom-call(bf16[32,128,256]{2,1,0:T(8,128)(2,1)} %image.1, bf16[256,1024]{1,0:T(8,128)(2,1)} %w_expand.1, bf16[3,3,1024]{2,1,0:T(4,128)(2,1)} %depth.1, bf16[1024,256]{1,0:T(8,128)(2,1)} %w_project.1, bf16[256,768]{1,0:T(8,128)(2,1)} %b_qkv.1, bf16[256,256]{1,0:T(8,128)(2,1)} %b_out.1, ...), custom_call_target="tpu_custom_call" | custom-call | tf_op jit(solution)/shard_map/pallas_call | solution.py:358
  162.7 3.1 %copy.20 = bf16[32,128,256]{2,1,0:T(8,128)(2,1)} copy(bf16[32,128,256]{2,1,0:T(8,128)(2,1)} %shard_map.100) | data formatting | bytes 4194304
  (4 shorter events, 0.1 us)
Async XLA Ops:
  0.0 2.0 %copy-start = (f32[8,64,64]{2,1,0:T(8,128)S(1)}, f32[8,64,64]{2,1,0:T(8,128)}, u32[]{:S(2)}) copy-start(f32[8,64,64]{2,1,0:T(8,128)} %param.19) | copy-start | bytes 393220

commit v2 on v1

--- a/solution.py
+++ b/solution.py
@@ -87,7 +87,7 @@
 
 
 def attention(tok, res, w_qkv, w_out, bias, ones):
-    lane = lax.broadcasted_iota(jnp.int32, (64, 128), 1)
+    lane = lax.broadcasted_iota(jnp.int32, (256, 128), 1)
     mlane = lax.broadcasted_iota(jnp.int32, (16, 128), 1)
     masks = [(mlane // HEAD_DIM == h).astype(F32).astype(BF) for h in range(4)]
     zero = jnp.zeros((16, 128), BF)
@@ -99,19 +99,18 @@
         q = (qkv[:, :WIDTH] * (LOG2E / HEAD_DIM**0.5)).astype(BF)
         k = qkv[:, WIDTH : 2 * WIDTH].astype(BF)
         v = qkv[:, 2 * WIDTH :].astype(BF)
-        mixed = []
-        for g in range(4):
-            rows = slice(64 * g, 64 * g + 64)
-            z = dot_nt(q[rows], spread(k[rows], masks, zero)) + bias[...]
-            tiles = [z[:, 128 * n : 128 * n + 128] for n in range(4)]
-            m = jnp.maximum(jnp.maximum(tiles[0], tiles[1]), jnp.maximum(tiles[2], tiles[3]))
-            for bit in (8, 4, 2, 1):
-                m = jnp.maximum(m, jnp.take_along_axis(m, lane ^ bit, axis=1))
-            p = jnp.concatenate([jnp.exp2(x - m).astype(BF) for x in tiles], axis=1)
-            num = dot(p, spread(v[rows], masks, zero))
-            den = dot(p, ones[...])
-            mixed.append((num / den).astype(BF))
-        out = dot(jnp.concatenate(mixed, axis=0), w_out[...]) + t
+        groups = [slice(64 * g, 64 * g + 64) for g in range(4)]
+        scores = [dot_nt(q[rows], spread(k[rows], masks, zero)) + bias[...] for rows in groups]
+        z = jnp.concatenate(scores, axis=0)
+        tiles = [z[:, 128 * n : 128 * n + 128] for n in range(4)]
+        m = jnp.maximum(jnp.maximum(tiles[0], tiles[1]), jnp.maximum(tiles[2], tiles[3]))
+        for bit in (8, 4, 2, 1):
+            m = jnp.maximum(m, jnp.take_along_axis(m, lane ^ bit, axis=1))
+        p = jnp.concatenate([jnp.exp2(x - m).astype(BF) for x in tiles], axis=1)
+        den = dot(p, ones[...])
+        num = jnp.concatenate([dot(p[rows], spread(v[rows], masks, zero)) for rows in groups], axis=0)
+        mixed = (num / den).astype(BF)
+        out = dot(mixed, w_out[...]) + t
         res[pl.ds(4 * c, 4)] = out.astype(BF).reshape(4, 64, WIDTH)
         return carry
 

time: 166 us -> 128 us (0.77)
  Pallas kernels: 160 us -> 122 us
    pallas_call x1, Pallas kernels: 160 us -> 122 us  [on_device(): pl.pallas_call(kernel, out_shape=jax.ShapeDtypeStruct(image.shape, BF), i...]
where the time goes in v2:
time: 128 us
  Pallas kernels  122 us (95%)
  local copies, waits for them, and re-layouts  5.98 us (5%)
    pallas_call x1, Pallas kernels, on_device(): pl.pallas_call(kernel, out_shape=jax.ShapeDtypeStruct(image.shape, BF), i...  122 us
    unnamed x5, local copies, waits for them, and re-layouts  4.38 us

profile of v2, /device:TPU:1, one launch (start us, length us, event | category | flops | bytes accessed | tf_op | source)
XLA Modules:
  0.0 128.0 jit_solution(5688014109824214104)
XLA Ops:
  0.0 0.0 copy-start
  0.0 1.1 copy.13
  1.2 0.8 copy.17.b_bias
  2.0 0.0 copy-done
  2.0 0.1 copy.15
  2.2 0.8 copy.18.g_bias
  2.9 121.9 %shard_map.100 = bf16[32,128,256]{2,1,0:T(8,128)(2,1)} custom-call(bf16[32,128,256]{2,1,0:T(8,128)(2,1)} %image.1, bf16[256,1024]{1,0:T(8,128)(2,1)} %w_expand.1, bf16[3,3,1024]{2,1,0:T(4,128)(2,1)} %depth.1, bf16[1024,256]{1,0:T(8,128)(2,1)} %w_project.1, bf16[256,768]{1,0:T(8,128)(2,1)} %b_qkv.1, bf16[256,256]{1,0:T(8,128)(2,1)} %b_out.1, ...), custom_call_target="tpu_custom_call" | custom-call | tf_op jit(solution)/shard_map/pallas_call | solution.py:357
  124.9 3.1 %copy.20 = bf16[32,128,256]{2,1,0:T(8,128)(2,1)} copy(bf16[32,128,256]{2,1,0:T(8,128)(2,1)} %shard_map.100) | data formatting | bytes 4194304
  (4 shorter events, 0.1 us)
Async XLA Ops:
  0.0 2.0 %copy-start = (f32[8,64,64]{2,1,0:T(8,128)S(1)}, f32[8,64,64]{2,1,0:T(8,128)}, u32[]{:S(2)}) copy-start(f32[8,64,64]{2,1,0:T(8,128)} %param.19) | copy-start | bytes 393220

commit v3 on v2

--- a/solution.py
+++ b/solution.py
@@ -75,22 +75,19 @@
     return (src == want).astype(F32).astype(BF)
 
 
-def spread(x, masks, zero):
-    parts = []
-    for t in range(4):
-        lo, hi = x[16 * t : 16 * t + 16, :128], x[16 * t : 16 * t + 16, 128:]
-        for h in range(4):
-            parts.append(jnp.concatenate([lo * masks[h], zero], axis=1))
-        for h in range(4):
-            parts.append(jnp.concatenate([zero, hi * masks[h]], axis=1))
-    return jnp.concatenate(parts, axis=0)
+def spread(x, masks):
+    return jnp.concatenate(
+        [x[16 * t : 16 * t + 16] * masks[h] for t in range(4) for h in range(4)], axis=0
+    )
 
 
 def attention(tok, res, w_qkv, w_out, bias, ones):
     lane = lax.broadcasted_iota(jnp.int32, (256, 128), 1)
+    high = lane >= 64
     mlane = lax.broadcasted_iota(jnp.int32, (16, 128), 1)
     masks = [(mlane // HEAD_DIM == h).astype(F32).astype(BF) for h in range(4)]
-    zero = jnp.zeros((16, 128), BF)
+    groups = [slice(64 * g, 64 * g + 64) for g in range(4)]
+    halves = (slice(0, 128), slice(128, 256))
 
     def step(c, carry):
         t = tok[pl.ds(4 * c, 4)].reshape(256, WIDTH)
@@ -99,22 +96,31 @@
         q = (qkv[:, :WIDTH] * (LOG2E / HEAD_DIM**0.5)).astype(BF)
         k = qkv[:, WIDTH : 2 * WIDTH].astype(BF)
         v = qkv[:, 2 * WIDTH :].astype(BF)
-        groups = [slice(64 * g, 64 * g + 64) for g in range(4)]
-        scores = [dot_nt(q[rows], spread(k[rows], masks, zero)) + bias[...] for rows in groups]
-        z = jnp.concatenate(scores, axis=0)
-        tiles = [z[:, 128 * n : 128 * n + 128] for n in range(4)]
-        m = jnp.maximum(jnp.maximum(tiles[0], tiles[1]), jnp.maximum(tiles[2], tiles[3]))
+        tiles, tops = [], []
+        for n, half in enumerate(halves):
+            z = jnp.concatenate(
+                [dot_nt(q[g, half], spread(k[g, half], masks)) + bias[n] for g in groups], axis=0
+            )
+            tiles.append((z[:, :128], z[:, 128:]))
+            tops.append(jnp.maximum(z[:, :128], z[:, 128:]))
+        m = jnp.maximum(
+            jnp.where(high, tops[0], tops[1]), pltpu.roll(jnp.where(high, tops[1], tops[0]), 64, 1)
+        )
         for bit in (8, 4, 2, 1):
             m = jnp.maximum(m, jnp.take_along_axis(m, lane ^ bit, axis=1))
-        p = jnp.concatenate([jnp.exp2(x - m).astype(BF) for x in tiles], axis=1)
-        den = dot(p, ones[...])
-        num = jnp.concatenate([dot(p[rows], spread(v[rows], masks, zero)) for rows in groups], axis=0)
-        mixed = (num / den).astype(BF)
-        out = dot(mixed, w_out[...]) + t
+        other = pltpu.roll(m, 64, 1)
+        tops = (jnp.where(high, m, other), jnp.where(high, other, m))
+        mixed = []
+        for n, half in enumerate(halves):
+            p = jnp.concatenate([jnp.exp2(x - tops[n]).astype(BF) for x in tiles[n]], axis=1)
+            den = dot(p, ones[...])
+            num = jnp.concatenate([dot(p[g], spread(v[g, half], masks)) for g in groups], axis=0)
+            mixed.append((num / den).astype(BF))
+        out = dot(jnp.concatenate(mixed, axis=1), w_out[...]) + t
         res[pl.ds(4 * c, 4)] = out.astype(BF).reshape(4, 64, WIDTH)
         return carry
 
-    lax.fori_loop(0, 4, step, 0)
+    lax.fori_loop(0, 4, step, 0, unroll=4)
 
 
 def kernel(
@@ -144,18 +150,6 @@
         for c in (left, C, right):
             pl.semaphore_signal(barrier, inc=1, device_id={"row": r, "col": c}, device_id_type=MESH)
 
-    perms[0] = perm_image()
-    perms[1] = perm_image_back()
-    perms[2] = perm_swap()
-    perms[3] = perm_grid()
-    perms[4] = perm_grid_back()
-    row_head = (lax.broadcasted_iota(jnp.int32, (512, WIDTH), 0) // 16) % HEADS
-    lane_head = lax.broadcasted_iota(jnp.int32, (512, WIDTH), 1) // HEAD_DIM
-    ones[...] = (row_head == lane_head).astype(F32).astype(BF)
-    w_half[...] = w_expand[...] * jnp.asarray(0.5, BF)
-    for n in range(9):
-        tap = depth[n // 3, pl.ds(n % 3, 1), :].astype(F32) * 0.5
-        taps[n] = jnp.broadcast_to(tap, (16, EXPANDED)).astype(BF)
     row16 = lax.broadcasted_iota(jnp.int32, (32, 16, WIDTH), 1)
     edge_l[...] = jnp.sum(
         jnp.where(row16 == 0, image[:, 0:16, :].astype(F32), 0.0), axis=1
@@ -164,22 +158,6 @@
         jnp.where(row16 == 15, image[:, 112:128, :].astype(F32), 0.0), axis=1
     ).astype(BF)
 
-    def expand(tokens, row0, row1, keep):
-        x = dot(perms[0], tokens)
-        if keep is not None:
-            image_p[keep] = x.astype(BF)
-        normed = layer_norm(x).astype(BF)
-        for n in range(4):
-            ch = slice(256 * n, 256 * n + 256)
-            h = gelu_of_half(dot(normed, w_half[:, ch])).astype(BF)
-            hidden[row0, 1:9, :, ch] = h[:128].reshape(8, 16, 256)
-            hidden[row1, 1:9, :, ch] = h[128:].reshape(8, 16, 256)
-
-    def expand_image(b):
-        rows = image[pl.ds(2 * b, 2)].reshape(256, WIDTH)
-        expand(rows, 2 * b + 1, 2 * b + 2, b)
-
-    expand_image(0)
     pl.semaphore_wait(barrier, 37)
 
     def halo_copies():
@@ -204,7 +182,42 @@
     halos = halo_copies()
     for copy in halos:
         copy.start()
-    expand_image(1)
+    perms[0] = perm_image()
+    perms[1] = perm_image_back()
+    perms[2] = perm_swap()
+    perms[3] = perm_grid()
+    perms[4] = perm_grid_back()
+    row_head = (lax.broadcasted_iota(jnp.int32, (256, 128), 0) // 16) % 4
+    lane_head = lax.broadcasted_iota(jnp.int32, (256, 128), 1) // HEAD_DIM
+    ones[...] = (row_head == lane_head).astype(F32).astype(BF)
+    w_half[...] = w_expand[...] * jnp.asarray(0.5, BF)
+    for n in range(9):
+        tap = depth[n // 3, pl.ds(n % 3, 1), :].astype(F32) * 0.5
+        taps[n] = jnp.broadcast_to(tap, (16, EXPANDED)).astype(BF)
+
+    def expand(tokens, row0, row1, keep):
+        x = dot(perms[0], tokens)
+        if keep is not None:
+            image_p[keep] = x.astype(BF)
+        normed = layer_norm(x).astype(BF)
+        for n in range(4):
+            ch = slice(256 * n, 256 * n + 256)
+            h = gelu_of_half(dot(normed, w_half[:, ch])).astype(BF)
+            hidden[row0, 1:9, :, ch] = h[:128].reshape(8, 16, 256)
+            hidden[row1, 1:9, :, ch] = h[128:].reshape(8, 16, 256)
+
+    def expand_image(b):
+        rows = image[pl.ds(2 * b, 2)].reshape(256, WIDTH)
+        expand(rows, 2 * b + 1, 2 * b + 2, b)
+
+    def expand_images(first, last):
+        def each(b, carry):
+            expand_image(b)
+            return carry
+
+        lax.fori_loop(first, last, each, 0)
+
+    expand_images(0, 16)
     for copy in halos:
         copy.wait()
 
@@ -273,10 +286,6 @@
             def rows(n, carry):
                 b = 4 * k + n
 
-                @pl.when(b < 14)
-                def _():
-                    expand_image(b + 2)
-
                 edges(2 * b + 2)
                 edges(2 * b + 3)
                 first = convolve(b)
@@ -347,8 +356,8 @@
 
 
 def in_tiles(bias):
-    tiled = (bias * LOG2E).reshape(HEADS, 64, 4, 16).transpose(1, 2, 0, 3)
-    return tiled.reshape(64, 512)
+    tiled = (bias * LOG2E).reshape(2, 4, 64, 4, 16).transpose(0, 2, 3, 1, 4)
+    return tiled.reshape(2, 64, 256)
 
 
 def on_device(image, w_expand, depth, w_project, b_qkv, b_out, b_bias, g_qkv, g_out, g_bias):
@@ -379,7 +388,7 @@
             pltpu.VMEM((16, 64, WIDTH), F32),
             pltpu.VMEM((16, 64, WIDTH), BF),
             pltpu.VMEM((5, 256, 256), BF),
-            pltpu.VMEM((512, WIDTH), BF),
+            pltpu.VMEM((256, 128), BF),
             dma((8,)),
             dma((8,)),
             dma((4,)),

time: 128 us -> 116 us (0.906)
  Pallas kernels: 122 us -> 110 us
    pallas_call x1, Pallas kernels: 122 us -> 110 us  [on_device(): pl.pallas_call(kernel, out_shape=jax.ShapeDtypeStruct(image.shape, BF), i...]
where the time goes in v3:
time: 116 us
  Pallas kernels  110 us (95%)
  local copies, waits for them, and re-layouts  5.98 us (5%)
    pallas_call x1, Pallas kernels, on_device(): pl.pallas_call(kernel, out_shape=jax.ShapeDtypeStruct(image.shape, BF), i...  110 us
    unnamed x5, local copies, waits for them, and re-layouts  4.38 us

profile of v3, /device:TPU:1, one launch (start us, length us, event | category | flops | bytes accessed | tf_op | source)
XLA Modules:
  0.0 116.2 jit_solution(12935966673023831915)
XLA Ops:
  0.0 0.0 copy-start
  0.0 1.1 copy.13
  1.2 0.8 copy.17.b_bias
  2.0 0.0 copy-done
  2.0 0.1 copy.15
  2.2 0.8 copy.18.g_bias
  2.9 110.1 %shard_map.100 = bf16[32,128,256]{2,1,0:T(8,128)(2,1)} custom-call(bf16[32,128,256]{2,1,0:T(8,128)(2,1)} %image.1, bf16[256,1024]{1,0:T(8,128)(2,1)} %w_expand.1, bf16[3,3,1024]{2,1,0:T(4,128)(2,1)} %depth.1, bf16[1024,256]{1,0:T(8,128)(2,1)} %w_project.1, bf16[256,768]{1,0:T(8,128)(2,1)} %b_qkv.1, bf16[256,256]{1,0:T(8,128)(2,1)} %b_out.1, ...), custom_call_target="tpu_custom_call" | custom-call | tf_op jit(solution)/shard_map/pallas_call | solution.py:366
  113.0 3.1 %copy.20 = bf16[32,128,256]{2,1,0:T(8,128)(2,1)} copy(bf16[32,128,256]{2,1,0:T(8,128)(2,1)} %shard_map.100) | data formatting | bytes 4194304
  (4 shorter events, 0.1 us)
Async XLA Ops:
  0.0 2.0 %copy-start = (f32[8,64,64]{2,1,0:T(8,128)S(1)}, f32[8,64,64]{2,1,0:T(8,128)}, u32[]{:S(2)}) copy-start(f32[8,64,64]{2,1,0:T(8,128)} %param.19) | copy-start | bytes 393220

commit v4 on v3

--- a/solution.py
+++ b/solution.py
@@ -79,6 +79,21 @@
     return jnp.concatenate(
         [x[16 * t : 16 * t + 16] * masks[h] for t in range(4) for h in range(4)], axis=0
     )
+
+
+def bias_tiles(bias, out):
+    lane = lax.broadcasted_iota(jnp.int32, (64, 128), 1)
+    pad = jnp.zeros((64, 64), F32)
+    for n in range(2):
+        wide = [jnp.concatenate([bias[4 * n + h], pad], axis=1) * LOG2E for h in range(4)]
+        for pair in range(2):
+            total = jnp.zeros((64, 128), F32)
+            for t in range(2):
+                for h in range(4):
+                    to = 64 * t + 16 * h
+                    moved = pltpu.roll(wide[h], (to - 16 * (2 * pair + t)) % 128, 1)
+                    total = jnp.where((lane >= to) & (lane < to + 16), moved, total)
+            out[n, :, 128 * pair : 128 * pair + 128] = total
 
 
 def attention(tok, res, w_qkv, w_out, bias, ones):
@@ -127,25 +142,29 @@
     image, w_expand, depth, w_project, b_qkv, b_out, b_bias, g_qkv, g_out, g_bias,
     result,
     halo_tb, halo_l, halo_r, edge_l, edge_r, send1, recv1, send2, recv2,
-    hidden, image_p, w_half, taps, hid_l, hid_r, act, tok, res, perms, ones,
+    hidden, image_p, w_half, taps, hid_l, hid_r, act0, act1, tok, res, perms, ones, bias_w, bias_g,
     halo_send, halo_recv, send_sem1, recv_sem1, send_sem2, recv_sem2,
 ):
     R, C = lax.axis_index("row"), lax.axis_index("col")
-    plane, mine = R % 4, (R // 4) * 4 + C
-
-    def device(d):
-        return {"row": (d // 4) * 4 + plane, "col": d % 4}
+    mine = (R // 4) * 4 + C
+
+    def peers():
+        out = []
+        for i in (4, 3, 5, 2, 6, 1, 7, 0):
+            row = (R + 4 * i) % 32
+            for c in (2, 3, 1, 0):
+                if i or c:
+                    col = (C + c) % 4
+                    out.append(((row // 4) * 4 + col, {"row": row, "col": col}))
+        return out
 
     up, down = (R + 31) % 32, (R + 1) % 32
     left, right = (C + 3) % 4, (C + 1) % 4
 
     barrier = pltpu.get_barrier_semaphore()
 
-    def greet(n, carry):
-        pl.semaphore_signal(barrier, inc=1, device_id=device((mine + n) % 32), device_id_type=MESH)
-        return carry
-
-    lax.fori_loop(1, 32, greet, 0)
+    for _, to in peers():
+        pl.semaphore_signal(barrier, inc=1, device_id=to, device_id_type=MESH)
     for r in (up, down):
         for c in (left, C, right):
             pl.semaphore_signal(barrier, inc=1, device_id={"row": r, "col": c}, device_id_type=MESH)
@@ -190,6 +209,8 @@
     row_head = (lax.broadcasted_iota(jnp.int32, (256, 128), 0) // 16) % 4
     lane_head = lax.broadcasted_iota(jnp.int32, (256, 128), 1) // HEAD_DIM
     ones[...] = (row_head == lane_head).astype(F32).astype(BF)
+    bias_tiles(b_bias, bias_w)
+    bias_tiles(g_bias, bias_g)
     w_half[...] = w_expand[...] * jnp.asarray(0.5, BF)
     for n in range(9):
         tap = depth[n // 3, pl.ds(n % 3, 1), :].astype(F32) * 0.5
@@ -239,10 +260,13 @@
         from_right = pltpu.roll(hidden[r, 1].astype(F32), 15, 0)
         hidden[r, 9] = jnp.where(row_s == 15, hid_r[pl.ds(15 + r, 1), :], from_right).astype(BF)
 
-    for r in range(2):
+    def all_edges(r, carry):
         edges(r)
-
-    def convolve(b):
+        return carry
+
+    lax.fori_loop(0, 34, all_edges, 0)
+
+    def convolve(b, act):
         for row in range(2):
             for n in range(8):
                 ch = slice(128 * n, 128 * n + 128)
@@ -252,22 +276,21 @@
                         term = hidden[2 * b + row + dr, dc : dc + 8, :, ch] * taps[3 * dr + dc, :, ch]
                         total = term if total is None else total + term
                 act[128 * row : 128 * row + 128, ch] = gelu_of_half(total).reshape(128, 128)
+
+    def project(b, n, act):
         update = dot(act[...], w_project[...])
-        return (image_p[b].astype(F32) + update).astype(BF)
+        first = (image_p[b].astype(F32) + update).astype(BF)
+        tok[:, 16 * n : 16 * n + 16, :] = dot(perms[2], first).reshape(16, 16, WIDTH)
 
     def exchange(src_of, dst_of, send_sem, recv_sem):
         own = pltpu.make_async_copy(src_of(mine), dst_of(mine), recv_sem)
         own.start()
 
-        def send(n, carry):
-            d = (mine + n) % 32
+        for d, to in peers():
             pltpu.make_async_remote_copy(
                 src_ref=src_of(d), dst_ref=dst_of(mine), send_sem=send_sem, recv_sem=recv_sem,
-                device_id=device(d), device_id_type=MESH,
+                device_id=to, device_id_type=MESH,
             ).start()
-            return carry
-
-        lax.fori_loop(1, 32, send, 0)
 
     def image_part(buf, k):
         return lambda d: buf.at[8 * k + d // 4, pl.ds(2 * (d % 4), 2)]
@@ -283,18 +306,13 @@
     def band(k, carry):
         @pl.when(k < 4)
         def _():
-            def rows(n, carry):
-                b = 4 * k + n
-
-                edges(2 * b + 2)
-                edges(2 * b + 3)
-                first = convolve(b)
-                swapped = dot(perms[2], first).reshape(16, 16, WIDTH)
-                tok[:, pl.ds(pl.multiple_of(16 * n, 16), 16), :] = swapped
-                return carry
-
-            lax.fori_loop(0, 4, rows, 0)
-            attention(tok, res, b_qkv, b_out, b_bias, ones)
+            acts = (act0, act1)
+            for n in range(4):
+                convolve(4 * k + n, acts[n % 2])
+                if n:
+                    project(4 * k + n - 1, n - 1, acts[(n - 1) % 2])
+            project(4 * k + 3, 3, acts[1])
+            attention(tok, res, b_qkv, b_out, bias_w, ones)
 
             def store(n, x):
                 send1[pl.ds(8 * k + 2 * n, 2)] = x.reshape(2, 8, 16, WIDTH)
@@ -309,7 +327,7 @@
             for n in range(4):
                 x = recv1[g, 8 * n : 8 * n + 8].reshape(256, WIDTH)
                 tok[:, 16 * n : 16 * n + 16, :] = dot(perms[3], x).reshape(16, 16, WIDTH)
-            attention(tok, res, g_qkv, g_out, g_bias, ones)
+            attention(tok, res, g_qkv, g_out, bias_g, ones)
 
             def store(n, x):
                 send2[g, 8 * n : 8 * n + 8] = x.reshape(8, 2, 16, WIDTH)
@@ -323,16 +341,12 @@
         own = pltpu.make_async_copy(send2.at[g, mine], image_part(recv2, g)(mine), recv_sem2.at[g])
         own.start()
 
-        def send(n, carry):
-            d = (mine + n) % 32
+        for d, to in peers():
             pltpu.make_async_remote_copy(
                 src_ref=send2.at[g, d], dst_ref=image_part(recv2, g)(mine),
                 send_sem=send_sem2.at[g], recv_sem=recv_sem2.at[g],
-                device_id=device(d), device_id_type=MESH,
+                device_id=to, device_id_type=MESH,
             ).start()
-            return carry
-
-        lax.fori_loop(1, 32, send, 0)
 
     lax.fori_loop(0, 5, band, 0)
 
@@ -353,11 +367,6 @@
         return carry
 
     lax.fori_loop(0, 4, drain, 0)
-
-
-def in_tiles(bias):
-    tiled = (bias * LOG2E).reshape(2, 4, 64, 4, 16).transpose(0, 2, 3, 1, 4)
-    return tiled.reshape(2, 64, 256)
 
 
 def on_device(image, w_expand, depth, w_project, b_qkv, b_out, b_bias, g_qkv, g_out, g_bias):
@@ -385,10 +394,13 @@
             pltpu.VMEM((64, EXPANDED), F32),
             pltpu.VMEM((64, EXPANDED), F32),
             pltpu.VMEM((256, EXPANDED), BF),
+            pltpu.VMEM((256, EXPANDED), BF),
             pltpu.VMEM((16, 64, WIDTH), F32),
             pltpu.VMEM((16, 64, WIDTH), BF),
             pltpu.VMEM((5, 256, 256), BF),
             pltpu.VMEM((256, 128), BF),
+            pltpu.VMEM((2, 64, 256), F32),
+            pltpu.VMEM((2, 64, 256), F32),
             dma((8,)),
             dma((8,)),
             dma((4,)),
@@ -400,8 +412,7 @@
             collective_id=0, has_side_effects=True, vmem_limit_bytes=56 << 20
         ),
     )(
-        image, w_expand, depth, w_project, b_qkv, b_out, in_tiles(b_bias),
-        g_qkv, g_out, in_tiles(g_bias),
+        image, w_expand, depth, w_project, b_qkv, b_out, b_bias, g_qkv, g_out, g_bias
     )
 
 

time: 116 us -> 110 us (0.948)
  Pallas kernels: 110 us -> 106 us
  local copies, waits for them, and re-layouts: 5.98 us -> 3.13 us
    pallas_call x1, Pallas kernels: 110 us -> 106 us  [on_device(): pl.pallas_call(kernel, out_shape=jax.ShapeDtypeStruct(image.shape, BF), i...]
    reshape x2 -> x0, local copies, waits for them, and re-layouts: 1.56 us -> none  [in_tiles(): return tiled.reshape(2, 64, 256)]
    unnamed x5 -> x1, local copies, waits for them, and re-layouts: 4.38 us -> 3.13 us
where the time goes in v4:
time: 110 us
  Pallas kernels  106 us (96%)
  local copies, waits for them, and re-layouts  3.13 us (3%)
    pallas_call x1, Pallas kernels, on_device(): pl.pallas_call(kernel, out_shape=jax.ShapeDtypeStruct(image.shape, BF), i...  106 us
    unnamed x1, local copies, waits for them, and re-layouts  3.13 us

profile of v4, /device:TPU:1, one launch (start us, length us, event | category | flops | bytes accessed | tf_op | source)
XLA Modules:
  0.0 109.6 jit_solution(11907804047783649322)
XLA Ops:
  0.0 106.4 %shard_map.100 = bf16[32,128,256]{2,1,0:T(8,128)(2,1)} custom-call(bf16[32,128,256]{2,1,0:T(8,128)(2,1)} %image.1, bf16[256,1024]{1,0:T(8,128)(2,1)} %w_expand.1, bf16[3,3,1024]{2,1,0:T(4,128)(2,1)} %depth.1, bf16[1024,256]{1,0:T(8,128)(2,1)} %w_project.1, bf16[256,768]{1,0:T(8,128)(2,1)} %b_qkv.1, bf16[256,256]{1,0:T(8,128)(2,1)} %b_out.1, ...), custom_call_target="tpu_custom_call" | custom-call | tf_op jit(solution)/shard_map/pallas_call | solution.py:375
  106.5 3.1 %copy.12 = bf16[32,128,256]{2,1,0:T(8,128)(2,1)} copy(bf16[32,128,256]{2,1,0:T(8,128)(2,1)} %shard_map.100) | data formatting | bytes 4194304

commit v5 on v4

--- a/solution.py
+++ b/solution.py
@@ -104,20 +104,23 @@
     groups = [slice(64 * g, 64 * g + 64) for g in range(4)]
     halves = (slice(0, 128), slice(128, 256))
 
-    def step(c, carry):
+    def project(c):
         t = tok[pl.ds(4 * c, 4)].reshape(256, WIDTH)
-        normed = layer_norm(t).astype(BF)
-        qkv = dot(normed, w_qkv[...])
+        qkv = dot(layer_norm(t).astype(BF), w_qkv[...])
         q = (qkv[:, :WIDTH] * (LOG2E / HEAD_DIM**0.5)).astype(BF)
-        k = qkv[:, WIDTH : 2 * WIDTH].astype(BF)
-        v = qkv[:, 2 * WIDTH :].astype(BF)
-        tiles, tops = [], []
+        return q, qkv[:, WIDTH : 2 * WIDTH].astype(BF), qkv[:, 2 * WIDTH :].astype(BF)
+
+    def scores(q, k, v):
+        tiles = []
         for n, half in enumerate(halves):
             z = jnp.concatenate(
                 [dot_nt(q[g, half], spread(k[g, half], masks)) + bias[n] for g in groups], axis=0
             )
             tiles.append((z[:, :128], z[:, 128:]))
-            tops.append(jnp.maximum(z[:, :128], z[:, 128:]))
+        return v, tiles
+
+    def weigh(v, tiles):
+        tops = [jnp.maximum(*pair) for pair in tiles]
         m = jnp.maximum(
             jnp.where(high, tops[0], tops[1]), pltpu.roll(jnp.where(high, tops[1], tops[0]), 64, 1)
         )
@@ -125,17 +128,32 @@
             m = jnp.maximum(m, jnp.take_along_axis(m, lane ^ bit, axis=1))
         other = pltpu.roll(m, 64, 1)
         tops = (jnp.where(high, m, other), jnp.where(high, other, m))
+        return v, [
+            jnp.concatenate([jnp.exp2(x - tops[n]).astype(BF) for x in tiles[n]], axis=1)
+            for n in range(2)
+        ]
+
+    def mix(c, v, weights):
         mixed = []
         for n, half in enumerate(halves):
-            p = jnp.concatenate([jnp.exp2(x - tops[n]).astype(BF) for x in tiles[n]], axis=1)
+            p = weights[n]
             den = dot(p, ones[...])
             num = jnp.concatenate([dot(p[g], spread(v[g, half], masks)) for g in groups], axis=0)
             mixed.append((num / den).astype(BF))
-        out = dot(jnp.concatenate(mixed, axis=1), w_out[...]) + t
+        out = dot(jnp.concatenate(mixed, axis=1), w_out[...])
+        out = out + tok[pl.ds(4 * c, 4)].reshape(256, WIDTH)
         res[pl.ds(4 * c, 4)] = out.astype(BF).reshape(4, 64, WIDTH)
-        return carry
-
-    lax.fori_loop(0, 4, step, 0, unroll=4)
+
+    first, second, third = {}, {}, {}
+    for i in range(7):
+        if i < 4:
+            first[i] = project(i)
+        if 0 <= i - 1 < 4:
+            second[i - 1] = scores(*first[i - 1])
+        if 0 <= i - 2 < 4:
+            third[i - 2] = weigh(*second[i - 2])
+        if 0 <= i - 3 < 4:
+            mix(i - 3, *third[i - 3])
 
 
 def kernel(

time: 110 us -> 100 us (0.909)
  Pallas kernels: 106 us -> 96.9 us
    pallas_call x1, Pallas kernels: 106 us -> 96.9 us  [on_device(): pl.pallas_call(kernel, out_shape=jax.ShapeDtypeStruct(image.shape, BF), i...]
where the time goes in v5:
time: 100 us
  Pallas kernels  96.9 us (97%)
  local copies, waits for them, and re-layouts  3.13 us (3%)
    pallas_call x1, Pallas kernels, on_device(): pl.pallas_call(kernel, out_shape=jax.ShapeDtypeStruct(image.shape, BF), i...  96.9 us
    unnamed x1, local copies, waits for them, and re-layouts  3.13 us

profile of v5, /device:TPU:1, one launch (start us, length us, event | category | flops | bytes accessed | tf_op | source)
XLA Modules:
  0.0 100.1 jit_solution(10595461575796251850)
XLA Ops:
  0.0 96.9 %shard_map.100 = bf16[32,128,256]{2,1,0:T(8,128)(2,1)} custom-call(bf16[32,128,256]{2,1,0:T(8,128)(2,1)} %image.1, bf16[256,1024]{1,0:T(8,128)(2,1)} %w_expand.1, bf16[3,3,1024]{2,1,0:T(4,128)(2,1)} %depth.1, bf16[1024,256]{1,0:T(8,128)(2,1)} %w_project.1, bf16[256,768]{1,0:T(8,128)(2,1)} %b_qkv.1, bf16[256,256]{1,0:T(8,128)(2,1)} %b_out.1, ...), custom_call_target="tpu_custom_call" | custom-call | tf_op jit(solution)/shard_map/pallas_call | solution.py:393
  96.9 3.1 %copy.12 = bf16[32,128,256]{2,1,0:T(8,128)(2,1)} copy(bf16[32,128,256]{2,1,0:T(8,128)(2,1)} %shard_map.100) | data formatting | bytes 4194304

commit v6 on v5

--- a/solution.py
+++ b/solution.py
@@ -254,7 +254,7 @@
             expand_image(b)
             return carry
 
-        lax.fori_loop(first, last, each, 0)
+        lax.fori_loop(first, last, each, 0, unroll=4)
 
     expand_images(0, 16)
     for copy in halos:

time: 100 us -> 98.2 us (0.982)
  Pallas kernels: 96.9 us -> 94.9 us
    pallas_call x1, Pallas kernels: 96.9 us -> 94.9 us  [on_device(): pl.pallas_call(kernel, out_shape=jax.ShapeDtypeStruct(image.shape, BF), i...]
where the time goes in v6:
time: 98.2 us; the launch traced here: 98 us
  Pallas kernels  94.9 us (97%)
  local copies, waits for them, and re-layouts  3.13 us (3%)
    pallas_call x1, Pallas kernels, on_device(): pl.pallas_call(kernel, out_shape=jax.ShapeDtypeStruct(image.shape, BF), i...  94.9 us
    unnamed x1, local copies, waits for them, and re-layouts  3.13 us

profile of v6, /device:TPU:1, one launch (start us, length us, event | category | flops | bytes accessed | tf_op | source)
XLA Modules:
  0.0 98.0 jit_solution(6388722031484685703)
XLA Ops:
  0.0 94.9 %shard_map.100 = bf16[32,128,256]{2,1,0:T(8,128)(2,1)} custom-call(bf16[32,128,256]{2,1,0:T(8,128)(2,1)} %image.1, bf16[256,1024]{1,0:T(8,128)(2,1)} %w_expand.1, bf16[3,3,1024]{2,1,0:T(4,128)(2,1)} %depth.1, bf16[1024,256]{1,0:T(8,128)(2,1)} %w_project.1, bf16[256,768]{1,0:T(8,128)(2,1)} %b_qkv.1, bf16[256,256]{1,0:T(8,128)(2,1)} %b_out.1, ...), custom_call_target="tpu_custom_call" | custom-call | tf_op jit(solution)/shard_map/pallas_call | solution.py:393
  94.9 3.1 %copy.12 = bf16[32,128,256]{2,1,0:T(8,128)(2,1)} copy(bf16[32,128,256]{2,1,0:T(8,128)(2,1)} %shard_map.100) | data formatting | bytes 4194304
